TPU v7x, 32 devices: a whole 2x2x4 slice. The times are simulated.
32 devices in a mesh: parts: 2 (over y), ship: 4 (over x, core), panel: 4 (over z).
Axes of the slice: x: 2, y: 2, z: 4, core: 2. Of those that a mesh axis runs over, the one named last changes fastest.
Arguments:
- right_side: float32 [8, 2, 32, 1024], P(('parts', 'ship'), None, None, 'panel'), parts along dimension 0, may hold values from -6 to 6
- current: bfloat16 [8, 2, 32, 1024], P(('parts', 'ship'), None, None, 'panel'), parts along dimension 0, may hold values from -6 to 6
- near_values: bfloat16 [8, 8, 6, 2, 128, 128], P(('parts', 'ship'), 'panel'), parts along dimension 0, may hold values from -0.15625 to 0.15625
- near_columns: int32 [8, 8, 6], P(('parts', 'ship'), 'panel'), parts along dimension 0, may hold values from 0 to 7, as said below
- block_inverse: bfloat16 [8, 8, 2, 128, 128], P(('parts', 'ship'), 'panel'), parts along dimension 0, may hold values from -1 to 2
- coupling_right: bfloat16 [8, 4, 2, 64, 1024], P('parts', 'ship', None, None, 'panel'), parts along dimension 0, may hold values from -0.125 to 0.125
- coupling_left: bfloat16 [8, 4, 2, 64, 1024], P(('parts', 'ship'), None, None, None, 'panel'), parts along dimension 0, may hold values from -0.26171875 to 0.26171875
- pair_rank: int32 [4, 4], replicated, may hold values from 32 to 64
- plan: int32 [3, 4], replicated, may hold values from 0 to 3, as said below
Outputs:
- field: float32 [8, 2, 32, 1024], P(('parts', 'ship'), None, None, 'panel'), parts along dimension 0
There are 2 independent parts, one for each index of `parts`. A program takes and returns all parts, laid end to end along the dimension named above; an argument that names none is the same for every part. Nothing has to cross between parts.
Inputs may be any that keep to these rules, and one draw needn't show every extreme that they name: Each row is a pairing of the ships: plan[k, plan[k, s]] = s and plan[k, s] != s; every two ships are paired in exactly one round. `near_columns`: the entries of one block row are distinct and differ from the row's own block.
All inputs are finite; a program needn't handle non-finite values.
Results may differ from a plain program's by a relative error of at most 0.0046.
Values may be sent and summed in bfloat16 or wider, within the bound.
A program may use at most 64 MiB of HBM per device.

v0:
```python
import jax
import jax.numpy as jnp
from jax import lax
from jax.sharding import PartitionSpec as P


def pair_up(product, rhs_count):
    real_src = product[:, :rhs_count]
    imag_src = product[:, rhs_count:]
    return jnp.stack([real_src[0] - imag_src[1], imag_src[0] + real_src[1]])


def near_field(values, columns, gathered):
    rhs_count = gathered.shape[1]
    block_len = values.shape[-1]
    cell_rows = gathered.reshape(2 * rhs_count, -1, block_len)
    picked = jnp.take(cell_rows, columns, axis=1)
    product = jnp.einsum("cinu,inztu->zcit", picked, values, preferred_element_type=jnp.float32)
    return pair_up(product, rhs_count).reshape(2, rhs_count, -1)


def apply_inverse(inverse, rest):
    rhs_count = rest.shape[1]
    block_len = inverse.shape[-1]
    rounded = rest.astype(jnp.bfloat16).reshape(2 * rhs_count, -1, block_len)
    product = jnp.einsum("ciu,iztu->zcit", rounded, inverse, preferred_element_type=jnp.float32)
    return pair_up(product, rhs_count).reshape(2, rhs_count, -1)


def compress(right_basis, sent):
    rhs_count = sent.shape[1]
    flat = sent.reshape(2 * rhs_count, -1)
    grams = jnp.einsum("zan,cn->zac", right_basis, flat, preferred_element_type=jnp.float32)
    return jnp.stack(
        [
            grams[0, :, :rhs_count] - grams[1, :, rhs_count:],
            grams[0, :, rhs_count:] + grams[1, :, :rhs_count],
        ]
    )


def expand(received, left_basis):
    outer = jnp.einsum("yac,zan->yzcn", received, left_basis, preferred_element_type=jnp.float32)
    return jnp.stack([outer[0, 0] - outer[1, 1], outer[0, 1] + outer[1, 0]])


def on_device(
    right_side,
    current,
    near_values,
    near_columns,
    block_inverse,
    coupling_right,
    coupling_left,
    pair_rank,
    plan,
):
    gathered = lax.all_gather(current[0], "panel", axis=2, tiled=True)
    rest = right_side[0] - near_field(near_values[0], near_columns[0], gathered)
    iterate = apply_inverse(block_inverse[0], rest)
    own_ship = lax.axis_index("ship")
    ship_count = coupling_left.shape[1]
    rank_index = lax.iota(jnp.int32, coupling_left.shape[3])
    for round_index in range(plan.shape[0]):
        partner = plan[round_index, own_ship]
        right_basis = lax.dynamic_index_in_dim(coupling_right, partner, 0, keepdims=False)[0]
        partial_value = compress(right_basis, iterate.astype(jnp.bfloat16))
        slot_mask = (lax.iota(jnp.int32, ship_count) == partner).astype(jnp.float32)
        spread = slot_mask[:, None, None, None] * partial_value[None]
        summed = lax.psum(spread, ("ship", "panel"))
        incoming = lax.dynamic_index_in_dim(summed, own_ship, 0, keepdims=False)
        keep_mask = rank_index < pair_rank[own_ship, partner]
        received = jnp.where(keep_mask[None, :, None], incoming, jnp.float32(0.0)).astype(
            jnp.bfloat16
        )
        left_basis = lax.dynamic_index_in_dim(coupling_left[0], partner, 0, keepdims=False)
        rest = rest - expand(received, left_basis)
        iterate = apply_inverse(block_inverse[0], rest)
    return iterate[None]


def solution(mesh):
    placed = (
        P(("parts", "ship"), None, None, "panel"),
        P(("parts", "ship"), None, None, "panel"),
        P(("parts", "ship"), "panel", None, None, None, None),
        P(("parts", "ship"), "panel", None),
        P(("parts", "ship"), "panel", None, None, None),
        P("parts", "ship", None, None, "panel"),
        P(("parts", "ship"), None, None, None, "panel"),
        P(),
        P(),
    )
    return jax.shard_map(
        on_device,
        mesh=mesh,
        in_specs=placed,
        out_specs=P(("parts", "ship"), None, None, "panel"),
        check_vma=False,
    )
```

profile of v0, /device:TPU:0, one launch (start us, length us, event | category | flops | bytes accessed | tf_op | source)
XLA Modules:
  0.0 216.4 jit_solution(11564814818696903876)
XLA Ops:
  0.0 0.0 copy-start
  0.0 0.0 copy-start.5
  0.0 1.4 constant_dynamic-slice_fusion.1
  5.6 0.0 copy-start.6
  7.0 0.0 copy-done.6
  7.0 0.7 fusion.72
  7.6 0.5 iota_compare_fusion.2
  8.2 0.0 copy-done.5
  8.2 15.1 %all-gather = bf16[1,2,32,1024]{3,2,1,0:T(8,128)(2,1)S(1)} all-gather(bf16[1,2,32,256]{3,2,1,0:T(8,128)(2,1)S(1)} %copy-done.5), channel_id=2, replica_groups=mesh['parts'=2,'ship'=4,'panel'=4] {'panel'}, dimensions={3}, use_global_device_ids=true | all-gather | bytes 163840 | tf_op jit(solution)/shard_map/all_gather | solution.py:58
  23.3 0.0 copy-start.7
  23.3 0.6 copy-done.7
  24.0 0.1 reshape.255
  24.1 0.6 gather_fusion
  24.7 0.0 copy-done
  24.7 0.4 convolution_bitcast_fusion
  25.1 0.1 pad_maximum_fusion
  25.2 0.0 copy-start.4
  25.3 0.8 copy-done.4
  26.1 0.0 copy-start.1
  26.2 0.8 copy-done.1
  27.0 0.0 copy-start.2
  27.0 0.2 convolution_bitcast_fusion.4
  27.2 0.7 copy-done.2
  28.0 0.1 fusion.16
  28.1 0.0 copy-start.3
  28.2 0.6 compare_convert_fusion.2
  28.8 0.1 broadcast_multiply_fusion.2
  28.9 60.9 %psum.21 = bf16[4,2,64,32]{2,3,1,0:T(8,128)(2,1)S(1)} all-reduce(f32[4,2,64,32]{2,3,1,0:T(8,128)S(1)} %broadcast_multiply_fusion.2), channel_id=1, replica_groups=mesh['parts'=2,'ship'=4,'panel'=4] {'ship','panel'}, use_global_device_ids=true, to_apply=%region_0.1 | all-reduce | flops 16384 | bytes 98304 | tf_op jit(solution)/shard_map/psum | solution.py:70
  89.8 0.0 copy-done.3
  89.8 0.1 convolution_bitcast_fusion.7
  90.1 0.2 convolution_bitcast_fusion.3
  90.3 0.1 fusion.14
  90.5 0.6 compare_convert_fusion.1
  91.2 0.1 broadcast_multiply_fusion.1
  91.2 60.0 %psum.22 = bf16[4,2,64,32]{2,3,1,0:T(8,128)(2,1)S(1)} all-reduce(f32[4,2,64,32]{2,3,1,0:T(8,128)S(1)} %broadcast_multiply_fusion.1), channel_id=1, replica_groups=mesh['parts'=2,'ship'=4,'panel'=4] {'ship','panel'}, use_global_device_ids=true, to_apply=%region_1.2 | all-reduce | flops 16384 | bytes 98304 | tf_op jit(solution)/shard_map/psum | solution.py:70
  151.2 0.6 iota_compare_fusion.1
  151.8 0.1 convolution_bitcast_fusion.6
  152.1 0.2 convolution_bitcast_fusion.2
  152.4 0.1 fusion.12
  152.6 0.7 compare_convert_fusion
  153.2 0.1 broadcast_multiply_fusion
  153.3 61.3 %psum.23 = bf16[4,2,64,32]{2,3,1,0:T(8,128)(2,1)S(1)} all-reduce(f32[4,2,64,32]{2,3,1,0:T(8,128)S(1)} %broadcast_multiply_fusion), channel_id=1, replica_groups=mesh['parts'=2,'ship'=4,'panel'=4] {'ship','panel'}, use_global_device_ids=true, to_apply=%region_2.3 | all-reduce | flops 16384 | bytes 98304 | tf_op jit(solution)/shard_map/psum | solution.py:70
  214.6 0.6 iota_compare_fusion
  215.2 0.1 convolution_bitcast_fusion.5
  215.5 0.2 convolution_bitcast_fusion.1
  215.7 0.1 pad_maximum_fusion.4
  215.8 0.6 copy.68
  (47 shorter events, 0.9 us)
Async XLA Ops:
  0.0 24.7 %copy-start = (bf16[1,2,6,2,128,128]{5,4,3,2,1,0:T(8,128)(2,1)S(1)}, bf16[1,2,6,2,128,128]{5,4,3,2,1,0:T(8,128)(2,1)}, u32[]{:S(2)}) copy-start(bf16[1,2,6,2,128,128]{5,4,3,2,1,0:T(8,128)(2,1)} %param.11) | copy-start | bytes 2359300
  0.0 8.2 %copy-start.5 = (bf16[1,2,32,256]{3,2,1,0:T(8,128)(2,1)S(1)}, bf16[1,2,32,256]{3,2,1,0:T(8,128)(2,1)}, u32[]{:S(2)}) copy-start(bf16[1,2,32,256]{3,2,1,0:T(8,128)(2,1)} %param.10) | copy-start | bytes 98308
  5.6 1.3 copy-start.6
  23.3 0.7 copy-start.7
  25.2 0.8 copy-start.4
  26.1 0.9 copy-start.1
  27.0 0.9 copy-start.2
  28.1 61.7 %copy-start.3 = (bf16[1,4,2,64,256]{4,3,2,1,0:T(8,128)(2,1)S(1)}, bf16[1,4,2,64,256]{4,3,2,1,0:T(8,128)(2,1)}, u32[]{:S(2)}) copy-start(bf16[1,4,2,64,256]{4,3,2,1,0:T(8,128)(2,1)} %param.15) | copy-start | bytes 786436
where the time goes:
time: 217 us; the launch traced here: 216 us
  blocking collectives  197 us (91%)
  local copies, waits for them, and re-layouts  6.77 us (3%)
  between operations  6.03 us (3%)
  other arithmetic  4.55 us (2%)
    psum x3, blocking collectives, on_device(): summed = lax.psum(spread, ('ship', 'panel'))  182 us
    all_gather x1, blocking collectives, on_device(): gathered = lax.all_gather(current[0], 'panel', axis=2, tiled=True)  15.1 us

commit v1 on v0

--- a/solution.py
+++ b/solution.py
@@ -67,7 +67,11 @@
         partial_value = compress(right_basis, iterate.astype(jnp.bfloat16))
         slot_mask = (lax.iota(jnp.int32, ship_count) == partner).astype(jnp.float32)
         spread = slot_mask[:, None, None, None] * partial_value[None]
-        summed = lax.psum(spread, ("ship", "panel"))
+
+        def do_things(frame, device_axis):
+            return jnp.sum(lax.all_gather(frame, axis_name=device_axis), axis=0)
+
+        summed = do_things(spread, ("ship", "panel"))
         incoming = lax.dynamic_index_in_dim(summed, own_ship, 0, keepdims=False)
         keep_mask = rank_index < pair_rank[own_ship, partner]
         received = jnp.where(keep_mask[None, :, None], incoming, jnp.float32(0.0)).astype(

time: 217 us -> 171 us (0.79)
  blocking collectives: 197 us -> 15.3 us
  waiting for transfers between devices: 0 us -> 116 us
  between operations: 6.03 us -> 19.3 us
  other arithmetic: 4.55 us -> 13.6 us
    psum x3 -> x0, blocking collectives: 182 us -> none  [on_device(): summed = lax.psum(spread, ('ship', 'panel'))]
    all_gather x0 -> x3, waiting for transfers between devices: none -> 116 us  [do_things(): return jnp.sum(lax.all_gather(frame, axis_name=device_axis), axis=0)]
    reduce_sum x0 -> x3, other arithmetic: none -> 5.52 us  [do_things(): return jnp.sum(lax.all_gather(frame, axis_name=device_axis), axis=0)]
    unnamed x17 -> x11, local copies, waits for them, and re-layouts: 3.05 us -> 0.04 us
  transfers between devices with their start and end apart: 0 -> 3, of which waited for: 0 -> 3; matrix products, arithmetic and copies ran while one was open for 0% -> 2% of each run, Pallas kernels for 0% -> 0%
where the time goes in v1:
time: 171 us
  waiting for transfers between devices  116 us (68%)
  between operations  19.3 us (11%)
  blocking collectives  15.3 us (9%)
  other arithmetic  13.6 us (8%)
  local copies, waits for them, and re-layouts  4.64 us (3%)
  matrix products  1.89 us (1%)
    all_gather x3, waiting for transfers between devices, do_things(): return jnp.sum(lax.all_gather(frame, axis_name=device_axis), axis=0)  116 us
    all_gather x1, blocking collectives, on_device(): gathered = lax.all_gather(current[0], 'panel', axis=2, tiled=True)  15.3 us
    reduce_sum x3, other arithmetic, do_things(): return jnp.sum(lax.all_gather(frame, axis_name=device_axis), axis=0)  5.52 us
  transfers between devices with their start and end apart: 3, of which 3 were waited for; matrix products, arithmetic and copies ran while one was open for 2% of the time, Pallas kernels for 0%

profile of v1, /device:TPU:0, one launch (start us, length us, event | category | flops | bytes accessed | tf_op | source)
XLA Modules:
  0.0 170.7 jit_solution(3141194703118608187)
XLA Ops:
  6.5 0.0 copy-start
  6.5 0.0 copy-start.1
  6.5 0.0 copy-start.2
  6.5 0.0 all-gather.5.cloned.1.call-start
  6.5 0.8 compare_select_fusion
  7.3 0.7 compare_and_fusion
  8.0 1.5 constant_dynamic-slice_fusion.1
  10.9 0.7 compare_convert_fusion.2
  11.6 0.9 squeeze.48
  12.4 15.3 %all-gather = bf16[1,2,32,1024]{3,2,1,0:T(8,128)(2,1)S(1)} all-gather(bf16[1,2,32,256]{3,2,1,0:T(8,128)(2,1)} %param.10), channel_id=2, replica_groups=mesh['parts'=2,'ship'=4,'panel'=4] {'panel'}, dimensions={3}, use_global_device_ids=true | all-gather | bytes 163840 | tf_op jit(solution)/shard_map/all_gather | solution.py:58
  27.7 0.0 copy-start.4
  27.8 0.1 reshape.264
  27.9 0.6 gather_fusion
  28.4 0.0 copy-done
  28.5 0.4 convolution_bitcast_fusion
  28.8 0.0 copy-start.3
  28.9 0.1 pad_maximum_fusion
  29.1 0.0 copy-done.1
  29.1 0.2 convolution_bitcast_fusion.4
  30.0 0.0 copy-done.2
  30.0 0.1 fusion.16
  30.2 0.7 broadcast_multiply_fusion.2
  31.0 0.0 all-gather.5.cloned.1.call-update
  31.0 0.0 all-gather.7.cloned.1.call-start
  34.7 0.0 copy-done.4
  34.7 0.7 fusion.72
  35.4 0.6 compare_convert_fusion.1
  35.9 0.7 iota_compare_fusion.2
  36.6 37.2 %all-gather.5.cloned.1.call-done = f32[16,4,2,64,32]{3,4,2,1,0:T(8,128)} async-done(((f32[1,4,2,64,32]{3,4,2,1,0:T(8,128)}), f32[16,4,2,64,32]{3,4,2,1,0:T(8,128)}) %all-gather.5.cloned.1.call-update) | async-done | bytes 1048592 | tf_op jit(solution)/shard_map/all_gather | solution.py:72
  73.8 1.8 %reduce_sum.27 = bf16[4,2,64,32]{2,3,1,0:T(8,128)(2,1)S(1)} reduce(f32[16,4,2,64,32]{3,4,2,1,0:T(8,128)} %all-gather.5.cloned.1.call-done, f32[]{:T(128)} %constant.54.clone.1), dimensions={0}, to_apply=%region_0.1 | reduce | flops 245760 | bytes 1081348 | tf_op jit(solution)/shard_map/reduce_sum | solution.py:72
  75.7 0.0 copy-done.3
  75.7 0.1 convolution_bitcast_fusion.7
  76.0 0.2 convolution_bitcast_fusion.3
  76.2 0.1 fusion.14
  76.4 0.7 broadcast_multiply_fusion.1
  77.1 0.0 all-gather.7.cloned.1.call-update
  77.2 0.0 all-gather.9.cloned.1.call-start
  77.2 0.7 compare_convert_fusion
  77.9 0.6 iota_compare_fusion.1
  78.5 39.0 %all-gather.7.cloned.1.call-done = f32[16,4,2,64,32]{3,4,2,1,0:T(8,128)} async-done(((f32[1,4,2,64,32]{3,4,2,1,0:T(8,128)}), f32[16,4,2,64,32]{3,4,2,1,0:T(8,128)}) %all-gather.7.cloned.1.call-update) | async-done | bytes 1048592 | tf_op jit(solution)/shard_map/all_gather | solution.py:72
  117.5 1.8 %reduce_sum.28 = bf16[4,2,64,32]{2,3,1,0:T(8,128)(2,1)S(1)} reduce(f32[16,4,2,64,32]{3,4,2,1,0:T(8,128)} %all-gather.7.cloned.1.call-done, f32[]{:T(128)} %constant.54.clone.1), dimensions={0}, to_apply=%region_1.2 | reduce | flops 245760 | bytes 1081348 | tf_op jit(solution)/shard_map/reduce_sum | solution.py:72
  119.3 0.1 convolution_bitcast_fusion.6
  119.6 0.2 convolution_bitcast_fusion.2
  119.8 0.1 fusion.12
  120.0 0.7 broadcast_multiply_fusion
  120.8 0.0 all-gather.9.cloned.1.call-update
  120.8 0.6 iota_compare_fusion
  121.4 39.6 %all-gather.9.cloned.1.call-done = f32[16,4,2,64,32]{3,4,2,1,0:T(8,128)} async-done(((f32[1,4,2,64,32]{3,4,2,1,0:T(8,128)}), f32[16,4,2,64,32]{3,4,2,1,0:T(8,128)}) %all-gather.9.cloned.1.call-update) | async-done | bytes 1048592 | tf_op jit(solution)/shard_map/all_gather | solution.py:72
  161.0 1.8 %reduce_sum.29 = bf16[4,2,64,32]{2,3,1,0:T(8,128)(2,1)S(1)} reduce(f32[16,4,2,64,32]{3,4,2,1,0:T(8,128)} %all-gather.9.cloned.1.call-done, f32[]{:T(128)} %constant.54.clone.1), dimensions={0}, to_apply=%region_2.3 | reduce | flops 245760 | bytes 1081348 | tf_op jit(solution)/shard_map/reduce_sum | solution.py:72
  162.9 0.1 convolution_bitcast_fusion.5
  163.2 0.2 convolution_bitcast_fusion.1
  163.4 0.1 pad_maximum_fusion.4
  163.5 0.6 copy.101
  (44 shorter events, 0.8 us)
Async XLA Ops:
  6.5 21.9 %copy-start = (bf16[1,2,6,2,128,128]{5,4,3,2,1,0:T(8,128)(2,1)S(1)}, bf16[1,2,6,2,128,128]{5,4,3,2,1,0:T(8,128)(2,1)}, u32[]{:S(2)}) copy-start(bf16[1,2,6,2,128,128]{5,4,3,2,1,0:T(8,128)(2,1)} %param.11) | copy-start | bytes 2359300
  6.5 22.6 %copy-start.1 = (bf16[1,2,2,128,128]{4,3,2,1,0:T(8,128)(2,1)S(1)}, bf16[1,2,2,128,128]{4,3,2,1,0:T(8,128)(2,1)}, u32[]{:S(2)}) copy-start(bf16[1,2,2,128,128]{4,3,2,1,0:T(8,128)(2,1)} %param.13) | copy-start | bytes 393220
  6.5 23.5 %copy-start.2 = (bf16[4,1,2,64,256]{4,3,2,1,0:T(8,128)(2,1)S(1)}, bf16[4,1,2,64,256]{4,3,2,1,0:T(8,128)(2,1)}, u32[]{:S(2)}) copy-start(bf16[4,1,2,64,256]{4,3,2,1,0:T(8,128)(2,1)} %param.14) | copy-start | bytes 786436
  6.5 67.3 %all-gather.5.cloned.1.call-start = ((), (), s32[]{:S(2)}) async-start(), calls=%async_computation | async-start | bytes 2228224 | tf_op jit(solution)/shard_map/all_gather | solution.py:72
  27.7 7.0 %copy-start.4 = (s32[4,4]{1,0:T(4,128)S(1)}, s32[4,4]{1,0:T(4,128)}, u32[]{:S(2)}) copy-start(s32[4,4]{1,0:T(4,128)} %param.16) | copy-start | bytes 196
  28.8 46.8 %copy-start.3 = (bf16[1,4,2,64,256]{4,3,2,1,0:T(8,128)(2,1)S(1)}, bf16[1,4,2,64,256]{4,3,2,1,0:T(8,128)(2,1)}, u32[]{:S(2)}) copy-start(bf16[1,4,2,64,256]{4,3,2,1,0:T(8,128)(2,1)} %param.15) | copy-start | bytes 786436
  31.0 86.5 %all-gather.7.cloned.1.call-start = ((), (), s32[]{:S(2)}) async-start(), calls=%async_computation.1 | async-start | bytes 2228224 | tf_op jit(solution)/shard_map/all_gather | solution.py:72
  77.2 83.9 %all-gather.9.cloned.1.call-start = ((), (), s32[]{:S(2)}) async-start(), calls=%async_computation.2 | async-start | bytes 2228224 | tf_op jit(solution)/shard_map/all_gather | solution.py:72
Sparse Core Ops, SparseCore 0:
  31.1 42.6 all-gather.4
  77.3 40.1 all-gather.6
  120.9 40.0 all-gather.8
